TPU v7x, 256 devices: a whole 4x4x8 slice. The times are simulated.
256 devices in a mesh: dp: 4 (over x_lo, core), seq: 64 (over x_hi, z, y).
Axes of the slice: x: 4 (x_hi: 2, x_lo: 2; x = x_hi * 2 + x_lo), y: 4, z: 8, core: 2. Of those that a mesh axis runs over, the one named last changes fastest.
Arguments:
- tokens: bfloat16 [4, 64, 256, 1152], P('dp', 'seq'), parts along dimension 0, may hold values from -6 to 6
- w_qkv: bfloat16 [2, 1152, 3456], P(None, None, 'seq'), may hold values from -1 to 1
- w_out: bfloat16 [2, 1152, 1152], P(None, None, 'seq'), may hold values from -0.1875 to 0.1875
- mod_shift: float32 [2, 1152], replicated, may hold values from -3 to 3
- mod_scale: float32 [2, 1152], replicated, may hold values from 0.5 to 2
- mod_gate: float32 [2, 1152], replicated, may hold values from 0.5 to 1.5
Outputs:
- result: bfloat16 [4, 64, 256, 1152], P('dp', 'seq'), parts along dimension 0
There are 4 independent parts, one for each index of `dp`. A program takes and returns all parts, laid end to end along the dimension named above; an argument that names none is the same for every part. Nothing has to cross between parts.
All inputs are finite; a program needn't handle non-finite values.
Results may differ from a plain program's by a relative error of at most 0.017.
Values may be sent and summed in bfloat16 or wider, within the bound.
A program may use at most 128 MiB of HBM per device.

v0:
```python
import jax
import jax.numpy as jnp
from jax import lax
from jax.sharding import PartitionSpec as P

HEADS = 16


def modulate(rows, shift, scale):
    values = rows.astype(jnp.float32)
    mean = jnp.mean(values, axis=-1, keepdims=True)
    centred = values - mean
    spread = jnp.mean(centred * centred, axis=-1, keepdims=True)
    return (centred * lax.rsqrt(spread + 1e-06) * scale + shift).astype(jnp.bfloat16)


def attend_space(packed):
    outer, inner, triple = packed.shape
    width = triple // 3
    head_size = width // HEADS
    query = packed[:, :, :width].reshape(outer, inner, HEADS, head_size)
    keys = packed[:, :, width : 2 * width].reshape(outer, inner, HEADS, head_size)
    values = packed[:, :, 2 * width :].reshape(outer, inner, HEADS, head_size)
    scores = jnp.einsum(
        "blhd,bmhd->bhlm", query, keys, preferred_element_type=jnp.float32
    ) * head_size ** (-0.5)
    scores = scores - jnp.max(scores, axis=-1, keepdims=True)
    weights = jnp.exp(scores)
    weights = (weights / jnp.sum(weights, axis=-1, keepdims=True)).astype(jnp.bfloat16)
    mixed = jnp.einsum("bhlm,bmhd->blhd", weights, values, preferred_element_type=jnp.float32)
    return mixed.astype(jnp.bfloat16).reshape(outer, inner, width)


def attend_time(packed):
    clips, frames, local, triple = packed.shape
    width = triple // 3
    head_size = width // HEADS
    query = packed[..., :width].reshape(clips, frames, local, HEADS, head_size)
    keys = packed[..., width : 2 * width].reshape(clips, frames, local, HEADS, head_size)
    values = packed[..., 2 * width :].reshape(clips, frames, local, HEADS, head_size)
    scores = jnp.einsum(
        "cfphd,cgphd->cphfg", query, keys, preferred_element_type=jnp.float32
    ) * head_size ** (-0.5)
    scores = scores - jnp.max(scores, axis=-1, keepdims=True)
    weights = jnp.exp(scores)
    weights = (weights / jnp.sum(weights, axis=-1, keepdims=True)).astype(jnp.bfloat16)
    mixed = jnp.einsum("cphfg,cgphd->cfphd", weights, values, preferred_element_type=jnp.float32)
    return mixed.astype(jnp.bfloat16).reshape(clips, frames, local, width)


def per_device(tokens, w_qkv, w_out, mod_shift, mod_scale, mod_gate):
    clips, frames, patches, width = tokens.shape
    rows = clips * frames * patches
    flat = tokens.reshape(rows, width)
    normed_a = modulate(flat, mod_shift[0], mod_scale[0])
    qkv_a = (
        jnp.dot(
            normed_a,
            lax.all_gather(w_qkv[0], "seq", axis=1, tiled=True),
            preferred_element_type=jnp.float32,
        )
        .astype(jnp.bfloat16)
        .reshape(clips * frames, patches, 3 * width)
    )
    spatial = attend_space(qkv_a).reshape(rows, width)
    first = (
        flat.astype(jnp.float32)
        + mod_gate[0]
        * jnp.dot(
            spatial,
            lax.all_gather(w_out[0], "seq", axis=1, tiled=True),
            preferred_element_type=jnp.float32,
        )
    ).astype(jnp.bfloat16)
    normed_b = modulate(first, mod_shift[1], mod_scale[1])
    qkv_b = (
        jnp.dot(
            normed_b,
            lax.all_gather(w_qkv[1], "seq", axis=1, tiled=True),
            preferred_element_type=jnp.float32,
        )
        .astype(jnp.bfloat16)
        .reshape(clips, frames, patches, 3 * width)
    )
    by_patch = lax.all_to_all(qkv_b, "seq", split_axis=2, concat_axis=1, tiled=True)
    temporal = attend_time(by_patch)
    returned = lax.all_to_all(temporal, "seq", split_axis=1, concat_axis=2, tiled=True).reshape(
        rows, width
    )
    result = (
        first.astype(jnp.float32)
        + mod_gate[1]
        * jnp.dot(
            returned,
            lax.all_gather(w_out[1], "seq", axis=1, tiled=True),
            preferred_element_type=jnp.float32,
        )
    ).astype(jnp.bfloat16)
    return result.reshape(clips, frames, patches, width)


def solution(mesh):
    in_specs = (
        P("dp", "seq", None, None),
        P(None, None, "seq"),
        P(None, None, "seq"),
        P(),
        P(),
        P(),
    )
    out_specs = P("dp", "seq", None, None)
    return jax.shard_map(
        per_device, mesh=mesh, in_specs=in_specs, out_specs=out_specs, check_vma=False
    )
```

profile of v0, /device:TPU:39, one launch (start us, length us, event | category | flops | bytes accessed | tf_op | source)
XLA Modules:
  0.0 786.7 jit_solution(6693070859661407531)
XLA Ops:
  6.5 0.0 copy-start.2
  6.5 0.0 all-gather.11.cloned.1.call-start
  6.5 1.8 fusion.86
  8.3 0.0 all-gather.11.cloned.1.call-update
  8.4 0.0 all-gather.9.cloned.1.call-start
  8.4 2.3 fusion.85
  10.7 0.0 all-gather.9.cloned.1.call-update
  10.7 0.0 all-gather.13.cloned.1.call-start
  10.8 0.7 all-gather.13.cloned.1.call-update
  11.5 0.8 slice_reduce_fusion.2
  12.3 0.8 slice_reduce_fusion
  13.1 0.0 copy-done.2
  13.1 0.2 convert_reduce_fusion
  13.3 0.3 fusion.45
  13.6 127.6 %all-gather.11.cloned.1.call-done = bf16[1,1152,1152]{1,0,2:T(2,128)(2,1)} async-done(((bf16[1,1152,18]{1,0,2:T(2,128)(2,1)}), bf16[1,1152,1152]{1,0,2:T(2,128)(2,1)}) %all-gather.11.cloned.1.call-update) | async-done | bytes 2654224 | tf_op jit(solution)/shard_map/all_gather | solution.py:71
  141.2 12.2 %copy.68 = bf16[1,1152,1152]{2,1,0:T(8,128)(2,1)} copy(bf16[1,1152,1152]{1,0,2:T(2,128)(2,1)} %all-gather.11.cloned.1.call-done) | data formatting | bytes 5308416 | tf_op jit(solution)/shard_map/all_gather | solution.py:71
  153.4 193.2 %all-gather.9.cloned.1.call-done = bf16[1,1152,3456]{1,0,2:T(2,128)(2,1)} async-done(((bf16[1,1152,54]{1,0,2:T(2,128)(2,1)}), bf16[1,1152,3456]{1,0,2:T(2,128)(2,1)}) %all-gather.9.cloned.1.call-update) | async-done | bytes 7962640 | tf_op jit(solution)/shard_map/all_gather | solution.py:59
  346.6 34.6 %copy.63 = bf16[1,1152,3456]{2,1,0:T(8,128)(2,1)} copy(bf16[1,1152,3456]{1,0,2:T(2,128)(2,1)} %all-gather.9.cloned.1.call-done) | data formatting | bytes 15925248 | tf_op jit(solution)/shard_map/all_gather | solution.py:59
  381.2 6.0 fusion.15
  387.2 0.1 fusion.84
  387.3 0.2 copy.64
  387.6 0.2 copy.65
  387.8 0.2 copy.66
  388.1 3.5 fusion.87
  391.5 0.0 copy-start.1
  391.5 2.9 fusion.44
  394.4 0.2 copy-done.1
  394.5 1.2 fusion.88
  395.7 0.0 copy-start
  395.7 0.3 multiply_reduce_fusion.2
  396.0 154.1 %all-gather.13.cloned.1.call-done = bf16[1,1152,3456]{1,0,2:T(2,128)(2,1)} async-done(((bf16[1,1152,54]{1,0,2:T(2,128)(2,1)}), bf16[1,1152,3456]{1,0,2:T(2,128)(2,1)}) %all-gather.13.cloned.1.call-update) | async-done | bytes 7962640 | tf_op jit(solution)/shard_map/all_gather | solution.py:79
  550.1 34.5 %copy.69 = bf16[1,1152,3456]{2,1,0:T(8,128)(2,1)} copy(bf16[1,1152,3456]{1,0,2:T(2,128)(2,1)} %all-gather.13.cloned.1.call-done) | data formatting | bytes 15925248 | tf_op jit(solution)/shard_map/all_gather | solution.py:79
  584.6 0.0 copy-done
  584.6 5.9 fusion.12
  590.5 2.7 copy.111
  593.2 0.5 broadcast.69
  593.8 12.1 %reduce.23 = bf16[256,3456]{1,0:T(8,128)(2,1)} reduce(bf16[256,1,1,3456]{3,2,1,0:T(2,128)(2,1)S(1)} %bitcast.83, bf16[]{:T(256)} %broadcast.69), dimensions={1,2}, to_apply=%bitcast.82.reduce_sub_computation | reduce | bytes 3538946
  605.9 4.8 reshape.144
  610.7 11.7 %all-to-all-start = ((bf16[64,2,6912]{2,1,0:T(2,128)(2,1)}), bf16[64,2,6912]{2,1,0:T(2,128)(2,1)}, u32[]{:S(2)}, u32[]{:S(2)}) async-start(bf16[64,2,6912]{2,1,0:T(2,128)(2,1)} %reshape.144), calls=%async_computation | async-start | bytes 3538944 | tf_op jit(solution)/shard_map/all_to_all | solution.py:85
  622.4 0.0 all-gather.15.cloned.1.call-start
  622.5 0.5 all-gather.15.cloned.1.call-update
  623.0 40.9 %all-to-all-done = bf16[64,2,6912]{2,1,0:T(2,128)(2,1)} async-done(((bf16[64,2,6912]{2,1,0:T(2,128)(2,1)}), bf16[64,2,6912]{2,1,0:T(2,128)(2,1)}, u32[]{:S(2)}, u32[]{:S(2)}) %all-to-all-start) | async-done | bytes 1769504 | tf_op jit(solution)/shard_map/all_to_all | solution.py:85
  664.0 9.3 %reshape.145 = bf16[256,1,1,3456]{3,2,1,0:T(2,128)(2,1)S(1)} reshape(bf16[64,2,6912]{2,1,0:T(2,128)(2,1)} %all-to-all-done) | data formatting | bytes 3538944
  673.3 11.8 %bitcast_reduce_fusion = bf16[256,3456]{1,0:T(8,128)(2,1)} fusion(bf16[256,1,1,3456]{3,2,1,0:T(2,128)(2,1)S(1)} %reshape.145), kind=kLoop, calls=%fused_computation.80 | loop fusion | bytes 3538944 | tf_op jit(solution)/shard_map/all_to_all | solution.py:85
  685.1 3.1 all_to_all.7
  688.2 1.4 fusion.83
  689.6 3.8 reshape.133
  693.4 1.9 reshape.135
  695.3 1.9 reshape.134
  697.3 2.0 fusion.89
  699.2 0.0 copy-start.3
  699.3 2.7 fusion.49
  702.0 0.0 copy-done.3
  702.0 3.0 fusion.43
  704.9 0.7 copy.89
  705.6 2.5 reshape.136
  708.1 10.7 %all-to-all-start.1 = ((bf16[1,64,4,1152]{3,2,0,1:T(4,128)(2,1)}), bf16[1,64,4,1152]{3,2,0,1:T(4,128)(2,1)}, u32[]{:S(2)}, u32[]{:S(2)}) async-start(bf16[1,64,4,1152]{3,2,0,1:T(4,128)(2,1)} %reshape.136), calls=%async_computation.1 | async-start | bytes 1179648 | tf_op jit(solution)/shard_map/all_to_all | solution.py:87
  718.8 45.9 %all-gather.15.cloned.1.call-done = bf16[1,1152,1152]{1,0,2:T(2,128)(2,1)} async-done(((bf16[1,1152,18]{1,0,2:T(2,128)(2,1)}), bf16[1,1152,1152]{1,0,2:T(2,128)(2,1)}) %all-gather.15.cloned.1.call-update) | async-done | bytes 2654224 | tf_op jit(solution)/shard_map/all_gather | solution.py:95
  764.7 10.9 %copy.80 = bf16[1,1152,1152]{2,1,0:T(8,128)(2,1)S(1)} copy(bf16[1,1152,1152]{1,0,2:T(2,128)(2,1)} %all-gather.15.cloned.1.call-done) | data formatting | bytes 5308416 | tf_op jit(solution)/shard_map/all_gather | solution.py:95
  775.6 0.0 all-to-all-done.1
  775.6 1.5 reshape.127
  777.1 3.1 fusion.34
  (4 shorter events, 0.0 us)
Async XLA Ops:
  6.5 6.6 copy-start.2
  6.5 134.6 %all-gather.11.cloned.1.call-start = ((), (), s32[]{:S(2)}) async-start(), calls=%async_computation.3 | async-start | bytes 5391360 | tf_op jit(solution)/shard_map/all_gather | solution.py:71
  8.4 338.2 %all-gather.9.cloned.1.call-start = ((), (), s32[]{:S(2)}) async-start(), calls=%async_computation.2 | async-start | bytes 16174080 | tf_op jit(solution)/shard_map/all_gather | solution.py:59
  10.7 539.4 %all-gather.13.cloned.1.call-start = ((), (), s32[]{:S(2)}) async-start(), calls=%async_computation.4 | async-start | bytes 16174080 | tf_op jit(solution)/shard_map/all_gather | solution.py:79
  391.5 3.0 copy-start.1
  395.7 188.8 %copy-start = (f32[256,1152]{1,0:T(8,128)}, f32[256,1152]{1,0:T(8,128)S(1)}, u32[]{:S(2)}) copy-start(f32[256,1152]{1,0:T(8,128)S(1)} %get-tuple-element.24) | copy-start | bytes 3538948
  610.7 53.2 %all-to-all-start = ((bf16[64,2,6912]{2,1,0:T(2,128)(2,1)}), bf16[64,2,6912]{2,1,0:T(2,128)(2,1)}, u32[]{:S(2)}, u32[]{:S(2)}) async-start(bf16[64,2,6912]{2,1,0:T(2,128)(2,1)} %reshape.144), calls=%async_computation | async-start | bytes 3538944 | tf_op jit(solution)/shard_map/all_to_all | solution.py:85
  622.4 142.2 %all-gather.15.cloned.1.call-start = ((), (), s32[]{:S(2)}) async-start(), calls=%async_computation.5 | async-start | bytes 5391360 | tf_op jit(solution)/shard_map/all_gather | solution.py:95
  699.2 2.7 copy-start.3
  708.1 67.5 %all-to-all-start.1 = ((bf16[1,64,4,1152]{3,2,0,1:T(4,128)(2,1)}), bf16[1,64,4,1152]{3,2,0,1:T(4,128)(2,1)}, u32[]{:S(2)}, u32[]{:S(2)}) async-start(bf16[1,64,4,1152]{3,2,0,1:T(4,128)(2,1)} %reshape.136), calls=%async_computation.1 | async-start | bytes 1179648 | tf_op jit(solution)/shard_map/all_to_all | solution.py:87
Sparse Core Ops, SparseCore 0:
  11.1 130.0 all-gather.10
  144.7 201.8 all-gather.8
  350.1 199.9 all-gather.12
  626.7 137.9 all-gather.14
where the time goes:
time: 795 us; the launch traced here: 787 us
  waiting for transfers between devices  563 us (71%)
  local copies, waits for them, and re-layouts  145 us (18%)
  matrix products  30.2 us (4%)
  starting transfers between devices  22.5 us (3%)
  between operations  13.3 us (2%)
  other arithmetic  12.8 us (2%)
    all_gather x1, waiting for transfers between devices, per_device(): lax.all_gather(w_qkv[0], 'seq', axis=1, tiled=True)  193 us
    all_gather x1, waiting for transfers between devices, per_device(): lax.all_gather(w_qkv[1], 'seq', axis=1, tiled=True)  154 us
    all_gather x1, waiting for transfers between devices, per_device(): lax.all_gather(w_out[0], 'seq', axis=1, tiled=True)  128 us
    all_gather x1, waiting for transfers between devices, per_device(): lax.all_gather(w_out[1], 'seq', axis=1, tiled=True)  45.9 us
    all_to_all x1, waiting for transfers between devices, per_device(): lax.all_to_all(qkv_b, 'seq', split_axis=2, concat_axis=1, tiled=True)  40.9 us
    all_gather x1, local copies, waits for them, and re-layouts, per_device(): lax.all_gather(w_qkv[0], 'seq', axis=1, tiled=True)  34.6 us
    all_gather x1, local copies, waits for them, and re-layouts, per_device(): lax.all_gather(w_qkv[1], 'seq', axis=1, tiled=True)  34.5 us
  transfers between devices with their start and end apart: 6, of which 5 were waited for; matrix products, arithmetic and copies ran while one was open for 15% of the time, Pallas kernels for 0%

commit v1 on v0

v1 whole, which is shorter than its diff:
```python
import functools

import jax
import jax.numpy as jnp
from jax import lax
from jax.experimental import pallas as pl
from jax.experimental.pallas import tpu as pltpu
from jax.sharding import PartitionSpec as P

HEADS = 16
HEAD_DIM = 72
WIDTH = 1152
TOKENS = 256
THIRD = WIDTH // 3
LOG2E = 1.4426950408889634
MESH = pl.DeviceIdType.MESH

SLOT_ROWS = 144
QKV_COLS = 54
OUT_COLS = 18
PIECES = ((0, 48), (48, 32), (80, 32), (112, 32))
QKV_WINDOW = ((0, 0), (80, 10))
OUT_WINDOW = ((48, 6), (64, 8))


def normalise(values, shift, scale):
    mean = jnp.mean(values, axis=0, keepdims=True)
    centred = values - mean
    spread = jnp.mean(centred * centred, axis=0, keepdims=True)
    return (centred * lax.rsqrt(spread + 1e-06) * scale + shift).astype(jnp.bfloat16)


def kernel(
    x_ref, wqkv_ref, wout_ref, mod_ref, o_ref,
    slots, qkv, heads, mixed, xt, nt, ft, sel_out, sel_in,
    send_a, recv_a, send_b, recv_b,
    ring_send, ring_recv, opp_send, a2a_send, a2a_recv,
):
    dp = lax.axis_index("dp")
    seq = lax.axis_index("seq")
    core, xlo = dp % 2, dp // 2
    hi, z, y = seq // 32, (seq // 4) % 8, seq % 4
    other = 1 - core

    turn = (z + 24 - 3 * y) % 8
    place = other * (4 * z + (y + z) % 4) + core * (4 * (y + 4 * (turn // 4)) + turn % 4)

    def spot(n):
        n = (n + 64) % 32
        a, b = n // 4, n % 4
        zz = other * a + core * ((3 * a + b) % 8)
        yy = other * ((b + 32 - a) % 4) + core * (a % 4)
        return 4 * zz + yy

    def slot_of(n):
        return 32 * core + spot(n)

    forward = (dp, 32 * hi + spot(place + 1))
    backward = (dp, 32 * hi + spot(place + 31))
    sibling = (2 * xlo + other, seq)
    opposite = (2 * (1 - xlo) + core, 32 * (1 - hi) + 4 * z + y)
    own = 32 * core + 4 * z + y

    barrier = pltpu.get_barrier_semaphore()

    def greet(k, _):
        pl.semaphore_signal(barrier, inc=1, device_id=(dp, (seq + k) % 64), device_id_type=MESH)
        return 0

    lax.fori_loop(1, 64, greet, 0)
    pl.semaphore_signal(barrier, inc=1, device_id=sibling, device_id_type=MESH)
    pl.semaphore_signal(barrier, inc=1, device_id=opposite, device_id_type=MESH)

    rows = jnp.concatenate(
        [
            wqkv_ref[0].astype(jnp.float32).T,
            wout_ref[0].astype(jnp.float32).T,
            wout_ref[1].astype(jnp.float32).T,
            wqkv_ref[1].astype(jnp.float32).T,
        ],
        axis=0,
    ).astype(jnp.bfloat16)
    mine = 32 * hi + 4 * z + y
    slots[mine] = rows

    pl.semaphore_wait(barrier, 65)

    def part(slot, k):
        return slots.at[slot, pl.ds(PIECES[k][0], PIECES[k][1])]

    def push(slot, k, way, device):
        pltpu.make_async_remote_copy(
            src_ref=part(slot, k), dst_ref=part(slot, k),
            send_sem=ring_send.at[k, way], recv_sem=ring_recv.at[k, slot],
            device_id=device, device_id_type=MESH,
        ).start()

    def arrive(slot, k):
        pltpu.make_async_remote_copy(
            src_ref=part(slot, k), dst_ref=part(slot, k),
            send_sem=ring_send.at[k, 0], recv_sem=ring_recv.at[k, slot],
            device_id=sibling, device_id_type=MESH,
        ).wait_recv()

    def opp_copy(k):
        return pltpu.make_async_remote_copy(
            src_ref=part(mine, k), dst_ref=part(mine, k),
            send_sem=opp_send.at[k], recv_sem=ring_recv.at[k, mine],
            device_id=opposite, device_id_type=MESH,
        )

    @pl.when(hi == core)
    def _():
        for k in range(4):
            opp_copy(k).start()

    def ring_first(k):
        @pl.when(hi != core)
        def _():
            arrive(own, k)

        push(own, k, 0, forward)
        push(own, k, 1, backward)

        @pl.when(hi != core)
        def _():
            push(own, k, 2, sibling)

    def ring_steps(ks, lo, hi_):
        def step(t, _):
            for k in ks:
                slot = slot_of(place - t)
                arrive(slot, k)
                push(slot, k, 0, forward)
                push(slot, k, 2, sibling)
                slot = slot_of(place + t)
                arrive(slot, k)
                push(slot, k, 1, backward)
                push(slot, k, 2, sibling)
            return 0

        lax.fori_loop(lo, hi_, step, 0)

    def ring_last(ks):
        for k in ks:
            slot = slot_of(place - 15)
            arrive(slot, k)
            if k % 2 == 0:
                push(slot, k, 0, forward)
            push(slot, k, 2, sibling)
            slot = slot_of(place + 15)
            arrive(slot, k)
            if k % 2 == 1:
                push(slot, k, 1, backward)
            push(slot, k, 2, sibling)
        for k in ks:
            slot = slot_of(place + 16)
            arrive(slot, k)
            push(slot, k, 2, sibling)

    def from_sibling(ks):
        def step(t, _):
            slot = 32 * other + t
            for k in ks:

                @pl.when(jnp.logical_or(hi == core, t != 4 * z + y))
                def _():
                    arrive(slot, k)

            return 0

        lax.fori_loop(0, 32, step, 0)

    ring_first(0)
    ring_first(1)

    xt[...] = x_ref[...].astype(jnp.float32).T
    nt[...] = normalise(xt[...], mod_ref[:, 0:1], mod_ref[:, 2:3])

    def selection(shape, row_axis, by_frame):
        packed = lax.broadcasted_iota(jnp.int32, shape, row_axis)
        token = lax.broadcasted_iota(jnp.int32, shape, 1 - row_axis)
        s, r = packed // 16, packed % 16
        t, p = r // 4, r % 4
        at = 256 * t + (64 * p + s if by_frame else 4 * s + p)
        return jnp.where(jnp.logical_and(t < 3, at == token), 1.0, 0.0).astype(jnp.bfloat16)

    def pack(send_ref, by_frame):
        flat = jnp.concatenate([ft[0:THIRD], ft[THIRD : 2 * THIRD], ft[2 * THIRD :]], axis=1)
        packed = lax.dot_general(
            sel_out[by_frame], flat, (((1,), (1,)), ((), ())), preferred_element_type=jnp.float32
        )
        send_ref[...] = packed.astype(jnp.bfloat16).reshape(64, 16, THIRD)

    def unpack(recv_ref, by_frame):
        return jnp.dot(
            sel_in[by_frame], recv_ref[...].reshape(1024, THIRD), preferred_element_type=jnp.float32
        )

    for by_frame in (0, 1):
        sel_out[by_frame] = selection((1024, 768), 0, by_frame)
        sel_in[by_frame] = selection((768, 1024), 1, by_frame)

    def exchange(send_ref, recv_ref, which):
        def one(k, _):
            to = (seq + k) % 64
            pltpu.make_async_remote_copy(
                src_ref=send_ref.at[to], dst_ref=recv_ref.at[seq],
                send_sem=a2a_send.at[which], recv_sem=a2a_recv.at[which],
                device_id=(dp, to), device_id_type=MESH,
            ).start()
            return 0

        lax.fori_loop(1, 64, one, 0)
        recv_ref[seq] = send_ref[seq]

    def exchanged(send_ref, recv_ref, which):
        done = pltpu.make_async_remote_copy(
            src_ref=send_ref.at[pl.ds(0, 63)], dst_ref=recv_ref.at[pl.ds(0, 63)],
            send_sem=a2a_send.at[which], recv_sem=a2a_recv.at[which],
            device_id=sibling, device_id_type=MESH,
        )
        done.wait_send()
        done.wait_recv()

    def project_qkv(layer):
        first, offset = QKV_WINDOW[layer]

        def one(g, _):
            block = slots[pl.ds(8 * g, 8), pl.ds(first, 64)].reshape(512, WIDTH)
            got = jnp.dot(block, nt[...], preferred_element_type=jnp.float32)
            qkv[pl.ds(8 * g, 8)] = got.reshape(8, 64, TOKENS)
            return 0

        lax.fori_loop(0, 8, one, 0)

        def split(g, _):
            four = [qkv[4 * g + j] for j in range(4)]
            four = [f[offset : offset + QKV_COLS] for f in four]
            units = (
                jnp.concatenate([four[0], four[1][:18]], axis=0),
                jnp.concatenate([four[1][18:], four[2][:36]], axis=0),
                jnp.concatenate([four[2][36:], four[3]], axis=0),
            )
            for j, unit in enumerate(units):
                at = 3 * g + j
                factor = jnp.where(at < HEADS, HEAD_DIM**-0.5 * LOG2E, 1.0).astype(jnp.float32)
                heads[at] = (unit * factor).astype(jnp.bfloat16)
            return 0

        lax.fori_loop(0, 16, split, 0)

    def scores_of(h):
        return lax.dot_general(
            heads[HEADS + h], heads[h], (((0,), (0,)), ((), ())), preferred_element_type=jnp.float32
        )

    def mix(h, weights, total):
        got = jnp.dot(heads[2 * HEADS + h], weights, preferred_element_type=jnp.float32)
        mixed[pl.ds(pl.multiple_of(HEAD_DIM * h, 8), HEAD_DIM)] = got / total

    def attend_space(h):
        scores = scores_of(h)
        weights = jnp.exp2(scores - jnp.max(scores, axis=0, keepdims=True))
        total = jnp.sum(weights, axis=0, keepdims=True)
        mix(h, weights.astype(jnp.bfloat16), total)

    def attend_time(h):
        scores = scores_of(h)
        low = lax.broadcasted_iota(jnp.int32, (64, 128), 1) < 64
        near = jnp.concatenate(
            [
                jnp.where(low, scores[0:64, 0:128], scores[64:128, 0:128]),
                jnp.where(low, scores[128:192, 128:256], scores[192:256, 128:256]),
            ],
            axis=1,
        )
        weights = jnp.exp2(near - jnp.max(near, axis=0, keepdims=True))
        total = jnp.sum(weights, axis=0, keepdims=True)
        column = lax.broadcasted_iota(jnp.int32, (64, TOKENS), 1) // 64
        spread = jnp.concatenate([jnp.where(column == p, weights, 0.0) for p in range(4)], axis=0)
        mix(h, spread.astype(jnp.bfloat16), total)

    def project_out(layer):
        first, offset = OUT_WINDOW[layer]
        nt[...] = mixed[...].astype(jnp.bfloat16)

        def one(g, _):
            block = slots[pl.ds(8 * g, 8), pl.ds(first, 32)].reshape(256, WIDTH)
            got = jnp.dot(block, nt[...], preferred_element_type=jnp.float32).reshape(8, 32, TOKENS)
            got = jnp.concatenate([got[j, offset : offset + OUT_COLS] for j in range(8)], axis=0)
            at = pl.ds(pl.multiple_of(144 * g, 16), 144)
            ft[at] = (xt[at] + mod_ref[at, 4 + layer : 5 + layer] * got).astype(jnp.bfloat16)
            return 0

        lax.fori_loop(0, 8, one, 0)

    def over_heads(attend, lo, hi_):
        def one(h, _):
            attend(h)
            return 0

        lax.fori_loop(lo, hi_, one, 0)

    ring_steps((0, 1), 1, 15)
    ring_last((0, 1))
    ring_first(2)
    ring_first(3)
    from_sibling((0, 1))
    project_qkv(0)
    for q in range(4):
        over_heads(attend_space, 4 * q, 4 * q + 4)
        ring_steps((2, 3), 1 + q, 2 + q)
    project_out(0)
    pack(send_a, 0)
    exchange(send_a, recv_a, 0)
    ring_steps((2, 3), 5, 15)
    ring_last((2, 3))
    exchanged(send_a, recv_a, 0)

    got = unpack(recv_a, 1)
    for t in range(3):
        xt[THIRD * t : THIRD * (t + 1)] = got[TOKENS * t : TOKENS * (t + 1)].T
    nt[...] = normalise(xt[...], mod_ref[:, 1:2], mod_ref[:, 3:4])
    from_sibling((2, 3))
    project_qkv(1)
    over_heads(attend_time, 0, HEADS)
    project_out(1)
    pack(send_b, 1)
    exchange(send_b, recv_b, 1)
    exchanged(send_b, recv_b, 1)
    got = unpack(recv_b, 0)
    for t in range(3):
        o_ref[:, THIRD * t : THIRD * (t + 1)] = got[TOKENS * t : TOKENS * (t + 1)].astype(jnp.bfloat16)

    def sent(k, way, count):
        rows = pl.ds(PIECES[k][0], PIECES[k][1])
        pltpu.make_async_remote_copy(
            src_ref=slots.at[pl.ds(0, count), rows], dst_ref=slots.at[pl.ds(0, count), rows],
            send_sem=ring_send.at[k, way], recv_sem=ring_recv.at[k, 0],
            device_id=sibling, device_id_type=MESH,
        ).wait_send()

    for k in range(4):
        sent(k, 0, 16 - k % 2)
        sent(k, 1, 15 + k % 2)

        @pl.when(hi == core)
        def _():
            sent(k, 2, 31)
            opp_copy(k).wait_send()

        @pl.when(hi != core)
        def _():
            sent(k, 2, 32)


def per_device(tokens, w_qkv, w_out, mod_shift, mod_scale, mod_gate):
    mod = jnp.concatenate([mod_shift, mod_scale, mod_gate, jnp.zeros_like(mod_gate)], axis=0).T
    vmem = pl.BlockSpec(memory_space=pltpu.VMEM)
    result = pl.pallas_call(
        kernel,
        out_shape=jax.ShapeDtypeStruct((TOKENS, WIDTH), jnp.bfloat16),
        in_specs=[vmem] * 4,
        out_specs=vmem,
        scratch_shapes=[
            pltpu.VMEM((64, SLOT_ROWS, WIDTH), jnp.bfloat16),
            pltpu.VMEM((64, 64, TOKENS), jnp.float32),
            pltpu.VMEM((3 * HEADS, HEAD_DIM, TOKENS), jnp.bfloat16),
            pltpu.VMEM((WIDTH, TOKENS), jnp.float32),
            pltpu.VMEM((WIDTH, TOKENS), jnp.float32),
            pltpu.VMEM((WIDTH, TOKENS), jnp.bfloat16),
            pltpu.VMEM((WIDTH, TOKENS), jnp.bfloat16),
            pltpu.VMEM((2, 1024, 768), jnp.bfloat16),
            pltpu.VMEM((2, 768, 1024), jnp.bfloat16),
            pltpu.VMEM((64, 16, THIRD), jnp.bfloat16),
            pltpu.VMEM((64, 16, THIRD), jnp.bfloat16),
            pltpu.VMEM((64, 16, THIRD), jnp.bfloat16),
            pltpu.VMEM((64, 16, THIRD), jnp.bfloat16),
            pltpu.SemaphoreType.DMA((4, 3)),
            pltpu.SemaphoreType.DMA((4, 64)),
            pltpu.SemaphoreType.DMA((4,)),
            pltpu.SemaphoreType.DMA((2,)),
            pltpu.SemaphoreType.DMA((2,)),
        ],
        compiler_params=pltpu.CompilerParams(
            collective_id=0, has_side_effects=True, vmem_limit_bytes=60 * 2**20
        ),
        name="latte",
    )(tokens.reshape(TOKENS, WIDTH), w_qkv, w_out, mod)
    return result.reshape(tokens.shape)


def solution(mesh):
    in_specs = (
        P("dp", "seq", None, None),
        P(None, None, "seq"),
        P(None, None, "seq"),
        P(),
        P(),
        P(),
    )
    return jax.shard_map(
        per_device, mesh=mesh, in_specs=in_specs, out_specs=P("dp", "seq", None, None), check_vma=False
    )
```

time: 795 us -> 206 us (0.26)
  waiting for transfers between devices: 563 us -> 0 us
  Pallas kernels: 0 us -> 198 us
  local copies, waits for them, and re-layouts: 145 us -> 5.4 us
  matrix products: 30.2 us -> 0 us
  starting transfers between devices: 22.5 us -> 0 us
  between operations: 13.3 us -> 0.01 us
  other arithmetic: 12.8 us -> 0.8 us
    all_gather x4 -> x0, waiting for transfers between devices: 521 us -> none  [the longest x1 193 us: per_device(): lax.all_gather(w_qkv[0], 'seq', axis=1, tiled=True)]
    pallas_call x0 -> x1, Pallas kernels: none -> 198 us  [per_device(): pl.pallas_call(kernel, out_shape=jax.ShapeDtypeStruct((TOKENS, WIDTH), jn...]
    all_gather x4 -> x0, local copies, waits for them, and re-layouts: 92.1 us -> none  [the longest x1 34.6 us: per_device(): lax.all_gather(w_qkv[0], 'seq', axis=1, tiled=True)]
    all_to_all x2 -> x0, waiting for transfers between devices: 40.9 us -> none  [the longest x1 40.9 us: per_device(): lax.all_to_all(qkv_b, 'seq', split_axis=2, concat_axis=1, tiled=True)]
    dot_general x7 -> x0, matrix products: 24.7 us -> none  [the longest x1 6 us: per_device(): jnp.dot(normed_a, lax.all_gather(w_qkv[0], 'seq', axis=1, tiled=True), pr...]
    all_to_all x2 -> x0, starting transfers between devices: 22.4 us -> none  [the longest x1 11.7 us: per_device(): lax.all_to_all(qkv_b, 'seq', split_axis=2, concat_axis=1, tiled=True)]
    all_to_all x2 -> x0, local copies, waits for them, and re-layouts: 14.9 us -> none  [per_device(): lax.all_to_all(qkv_b, 'seq', split_axis=2, concat_axis=1, tiled=True)]
    unnamed x1 -> x0, other arithmetic: 12.1 us -> none
  transfers between devices with their start and end apart: 6 -> 0, of which waited for: 5 -> 0; matrix products, arithmetic and copies ran while one was open for 15% -> 0% of each run, Pallas kernels for 0% -> 0%
where the time goes in v1:
time: 206 us; the launch traced here: 204 us
  Pallas kernels  198 us (96%)
  local copies, waits for them, and re-layouts  5.4 us (3%)
    pallas_call x1, Pallas kernels, per_device(): pl.pallas_call(kernel, out_shape=jax.ShapeDtypeStruct((TOKENS, WIDTH), jn...  198 us
    unnamed x7, local copies, waits for them, and re-layouts  4.27 us

profile of v1, /device:TPU:39, one launch (start us, length us, event | category | flops | bytes accessed | tf_op | source)
XLA Modules:
  0.0 204.3 jit_solution(3763221726811727152)
XLA Ops:
  0.0 0.1 pad.3.clone
  0.1 0.8 maximum_maximum_fusion
  0.9 0.0 copy-start
  0.9 1.0 copy.12
  1.9 0.0 copy-done
  1.9 0.0 copy-start.1
  1.9 1.2 copy.13.wqkv_ref
  3.2 0.0 copy-done.1
  3.2 1.1 copy.14.wout_ref
  4.3 198.1 %latte.1 = bf16[256,1152]{1,0:T(8,128)(2,1)} custom-call(bf16[256,1152]{1,0:T(8,128)(2,1)} %bitcast.5, bf16[2,1152,54]{2,1,0:T(8,128)(2,1)} %copy.13.wqkv_ref, bf16[2,1152,18]{2,1,0:T(8,128)(2,1)} %copy.14.wout_ref, f32[1152,8]{1,0:T(8,128)} %bitcast.3), custom_call_target="tpu_custom_call" | custom-call | tf_op jit(solution)/shard_map/latte/pallas_call | solution.py:361
  202.4 1.9 copy.16
  (1 shorter events, 0.0 us)
Async XLA Ops:
  0.9 1.1 copy-start
  1.9 1.2 copy-start.1

commit v2 on v1

v2 whole, which is shorter than its diff:
```python
import functools

import jax
import jax.numpy as jnp
from jax import lax
from jax.experimental import pallas as pl
from jax.experimental.pallas import tpu as pltpu
from jax.sharding import PartitionSpec as P

HEADS = 16
HEAD_DIM = 72
WIDTH = 1152
TOKENS = 256
THIRD = WIDTH // 3
LOG2E = 1.4426950408889634
MESH = pl.DeviceIdType.MESH

SLOT_ROWS = 144
QKV_COLS = 54
OUT_COLS = 18
PIECES = (
    (0, 32, "z", False),
    (32, 16, "y", False),
    (48, 16, "z", True),
    (64, 16, "y", True),
    (80, 32, "z", False),
    (112, 16, "y", False),
    (128, 16, "y", True),
)
LAYER_PIECES = ((0, 1, 2, 3), (4, 5, 6))
ORDER = (
    32, 0, 64, 96, 33, 7, 71, 103, 1, 65, 24, 88, 39, 8, 56, 97, 40, 120, 72, 104, 6, 31, 2, 66,
    70, 34, 63, 38, 102, 98, 57, 112, 89, 16, 95, 47, 73, 25, 79, 80, 41, 5, 15, 48, 3, 127, 121, 111,
    30, 105, 67, 69, 14, 99, 10, 37, 35, 26, 94, 78, 58, 62, 101, 9, 23, 42, 46, 87, 49, 74, 122, 55,
    90, 126, 4, 119, 59, 110, 13, 106, 68, 17, 11, 81, 43, 113, 36, 123, 50, 18, 77, 29, 107, 27, 75, 91,
    100, 22, 60, 45, 54, 125, 86, 114, 61, 93, 82, 51, 28, 118, 12, 109, 21, 44, 53, 115, 76, 92, 19, 128,
    83, 160, 117, 192, 108, 124, 85, 20, 52, 84, 116, 135, 129, 152, 136, 199, 193, 167, 161, 216, 200, 184, 168, 159,
    153, 143, 134, 130, 137, 198, 166, 162, 144, 194, 223, 217, 191, 185, 208, 207, 176, 201, 142, 175, 169, 151, 138, 145,
    158, 133, 131, 197, 163, 154, 195, 222, 165, 186, 218, 215, 209, 190, 177, 150, 206, 202, 157, 170, 146, 183, 155, 174,
    141, 139, 187, 196, 132, 219, 164, 178, 210, 189, 171, 149, 221, 203, 182, 147, 188, 214, 173, 205, 156, 179, 172, 140,
    211, 181, 220, 213, 204, 212, 148, 180,
)
UP_Y, DOWN_Y, UP_Z, DOWN_Z, SIBLING, OPPOSITE = range(6)
QKV_WINDOW = ((0, 0), (80, 10))
OUT_WINDOW = ((48, 6), (64, 8))


def normalise(values, shift, scale):
    mean = jnp.mean(values, axis=0, keepdims=True)
    centred = values - mean
    spread = jnp.mean(centred * centred, axis=0, keepdims=True)
    return (centred * lax.rsqrt(spread + 1e-06) * scale + shift).astype(jnp.bfloat16)


def kernel(
    x_ref, wqkv_ref, wout_ref, shift_ref, scale_ref, gate_ref, o_ref,
    slots, mod, qkv, heads, mixed, xt, nt, ft, sel_out, sel_in,
    send_a, recv_a, send_b, recv_b,
    ring_send, ring_recv, a2a_send, a2a_recv,
):
    dp = lax.axis_index("dp")
    seq = lax.axis_index("seq")
    core, xlo = dp % 2, dp // 2
    hi, z, y = seq // 32, (seq // 4) % 8, seq % 4
    other = 1 - core

    def chip(yy, zz):
        return (dp, 32 * hi + 4 * ((zz + 8) % 8) + (yy + 4) % 4)

    sibling = (2 * xlo + other, seq)
    opposite = (2 * (1 - xlo) + core, 32 * (1 - hi) + 4 * z + y)
    devices = (chip(y + 1, z), chip(y - 1, z), chip(y, z + 1), chip(y, z - 1), sibling, opposite)

    barrier = pltpu.get_barrier_semaphore()

    def greet(k, _):
        pl.semaphore_signal(barrier, inc=1, device_id=(dp, (seq + k) % 64), device_id_type=MESH)
        return 0

    lax.fori_loop(1, 64, greet, 0)
    pl.semaphore_signal(barrier, inc=1, device_id=sibling, device_id_type=MESH)
    pl.semaphore_signal(barrier, inc=1, device_id=opposite, device_id_type=MESH)

    columns = wqkv_ref[...].astype(jnp.float32)
    outs = wout_ref[...].astype(jnp.float32)
    rows = jnp.concatenate([columns[:, 0], outs[:, 0], outs[:, 1], columns[:, 1]], axis=0).astype(jnp.bfloat16)
    mine = 32 * hi + 4 * z + y
    slots[mine] = rows

    pl.semaphore_wait(barrier, 65)

    def part(slot, k):
        return slots.at[slot, pl.ds(PIECES[k][0], PIECES[k][1])]

    def push(slot, k, way):
        pltpu.make_async_remote_copy(
            src_ref=part(slot, k), dst_ref=part(slot, k),
            send_sem=ring_send.at[k, way], recv_sem=ring_recv.at[k, slot],
            device_id=devices[way], device_id_type=MESH,
        ).start()

    def arrive(slot, k):
        pltpu.make_async_remote_copy(
            src_ref=part(slot, k), dst_ref=part(slot, k),
            send_sem=ring_send.at[k, 0], recv_sem=ring_recv.at[k, slot],
            device_id=sibling, device_id_type=MESH,
        ).wait_recv()

    def routes(k, dy, dz):
        ways = []
        if PIECES[k][2] == "z":
            if dy == 0:
                ways += {0: [UP_Z, DOWN_Z], 3: [DOWN_Z] * (k % 2), 4: [], 5: [UP_Z] * (1 - k % 2)}.get(
                    dz, [DOWN_Z] if dz < 4 else [UP_Z]
                )
                ways += [UP_Y, DOWN_Y]
            elif dy != 2 and (dz + k) % 2 == dy // 2:
                ways += [DOWN_Y if dy == 1 else UP_Y]
        else:
            if dz == 0:
                ways += [UP_Z, DOWN_Z]
                if dy == 0:
                    ways += [UP_Y, DOWN_Y]
                elif dy != 2 and k % 2 == dy // 2:
                    ways += [DOWN_Y if dy == 1 else UP_Y]
            elif dz in (3, 5):
                if (dy + k) % 2 == dz // 4:
                    ways += [DOWN_Z if dz == 3 else UP_Z]
            elif dz != 4:
                ways += [DOWN_Z if dz < 4 else UP_Z]
        return ways

    def block_of(half, dy, dz):
        return 32 * half + 4 * lax.rem(z + dz, 8) + lax.rem(y + dy, 4)

    def event(k, dy, dz):
        slot = block_of(core, dy, dz)
        last = PIECES[k][3]
        start = dy == 0 and dz == 0

        def onward():
            for way in routes(k, dy, dz):
                push(slot, k, way)

        if start:

            @pl.when(hi != core)
            def _():
                arrive(slot, k)

            @pl.when(hi == core)
            def _():
                push(slot, k, OPPOSITE)
                if last:
                    onward()

            @pl.when(hi != core)
            def _():
                push(slot, k, SIBLING)

        else:
            arrive(slot, k)
            if last:

                @pl.when(hi == core)
                def _():
                    onward()
                    push(slot, k, OPPOSITE)

            push(slot, k, SIBLING)
        if not last:
            onward()

    def course(k):
        return [(k, dy, dz) for dy in range(4) for dz in range(8)]

    def run(events):
        for e in events:
            event(*e)

    def from_sibling(ks, dy, dz):
        slot = block_of(other, dy, dz)

        def taken():
            for k in ks:
                arrive(slot, k)

        if dy == 0 and dz == 0:
            pl.when(hi == core)(taken)
        else:
            taken()

    order = [(e // 32, e // 8 % 4, e % 8) for e in ORDER]
    end_a = 1 + max(i for i, e in enumerate(order) if e[0] in LAYER_PIECES[0])
    run(order[:4])

    def prepare():
        six = jnp.concatenate([shift_ref[...], scale_ref[...], gate_ref[...], gate_ref[...]], axis=0)
        mod[...] = six.T
        xt[...] = x_ref[...].astype(jnp.float32).T
        nt[...] = normalise(xt[...], mod[:, 0:1], mod[:, 2:3])

    def selected(shape, axis, start, by_frame):
        packed = lax.broadcasted_iota(jnp.int32, shape, axis) + start
        s, t, p = packed >> 4, (packed >> 2) & 3, packed & 3
        at = 256 * t + (64 * p + s if by_frame else 4 * s + p)
        return jnp.where(t < 3, at, -1)

    def make_sel_out(by_frame, q):
        at = selected((256, 1), 0, 256 * q, by_frame)
        token = lax.broadcasted_iota(jnp.int32, (256, 768), 1)
        sel_out[by_frame, 256 * q : 256 * (q + 1)] = jnp.where(at == token, 1.0, 0.0).astype(jnp.bfloat16)

    def make_sel_in(by_frame, q):
        at = selected((1, 1024), 1, 0, by_frame)
        token = lax.broadcasted_iota(jnp.int32, (256, 1024), 0) + 256 * q
        sel_in[by_frame, 256 * q : 256 * (q + 1)] = jnp.where(at == token, 1.0, 0.0).astype(jnp.bfloat16)

    def pack_and_send(send_ref, recv_ref, by_frame):
        flat = jnp.concatenate([ft[0:THIRD], ft[THIRD : 2 * THIRD], ft[2 * THIRD :]], axis=1)

        def quarter(c, _):
            q = lax.rem(seq // 16 + 1 + c, 4)
            packed = lax.dot_general(
                sel_out[by_frame, pl.ds(pl.multiple_of(256 * q, 256), 256)], flat,
                (((1,), (1,)), ((), ())), preferred_element_type=jnp.float32,
            )
            send_ref[pl.ds(16 * q, 16)] = packed.astype(jnp.bfloat16).reshape(16, 16, THIRD)

            def one(j, _):
                to = 16 * q + lax.rem(seq + j, 16)

                @pl.when(to != seq)
                def _():
                    pltpu.make_async_remote_copy(
                        src_ref=send_ref.at[to], dst_ref=recv_ref.at[seq],
                        send_sem=a2a_send.at[by_frame], recv_sem=a2a_recv.at[by_frame],
                        device_id=(dp, to), device_id_type=MESH,
                    ).start()

                return 0

            lax.fori_loop(0, 16, one, 0)
            return 0

        lax.fori_loop(0, 4, quarter, 0)
        recv_ref[seq] = send_ref[seq]

    def unpack(recv_ref, by_frame):
        return jnp.dot(
            sel_in[by_frame], recv_ref[...].reshape(1024, THIRD), preferred_element_type=jnp.float32
        )

    def exchanged(send_ref, recv_ref, which):
        done = pltpu.make_async_remote_copy(
            src_ref=send_ref.at[pl.ds(0, 63)], dst_ref=recv_ref.at[pl.ds(0, 63)],
            send_sem=a2a_send.at[which], recv_sem=a2a_recv.at[which],
            device_id=sibling, device_id_type=MESH,
        )
        done.wait_send()
        done.wait_recv()

    def project_slots(layer, slot_list):
        first = QKV_WINDOW[layer][0]
        block = jnp.concatenate([slots[j, pl.ds(first, 64)] for j in slot_list], axis=0)
        got = jnp.dot(block, nt[...], preferred_element_type=jnp.float32)
        for n, j in enumerate(slot_list):
            qkv[j] = got[64 * n : 64 * (n + 1)]

    def project_qkv(layer):
        def one(g, _):
            project_slots(layer, [8 * g + j for j in range(8)])
            return 0

        lax.fori_loop(0, 8, one, 0)

    def split_heads(layer, lo, hi_):
        offset = QKV_WINDOW[layer][1]

        def split(g, _):
            four = [qkv[4 * g + j, offset : offset + QKV_COLS] for j in range(4)]
            units = (
                jnp.concatenate([four[0], four[1][:18]], axis=0),
                jnp.concatenate([four[1][18:], four[2][:36]], axis=0),
                jnp.concatenate([four[2][36:], four[3]], axis=0),
            )
            for j, unit in enumerate(units):
                at = 3 * g + j
                factor = jnp.where(at < HEADS, HEAD_DIM**-0.5 * LOG2E, 1.0).astype(jnp.float32)
                heads[at] = (unit * factor).astype(jnp.bfloat16)
            return 0

        lax.fori_loop(lo, hi_, split, 0)

    def scores_of(h):
        return lax.dot_general(
            heads[HEADS + h], heads[h], (((0,), (0,)), ((), ())), preferred_element_type=jnp.float32
        )

    def mix(h, weights, total):
        got = jnp.dot(heads[2 * HEADS + h], weights, preferred_element_type=jnp.float32)
        mixed[pl.ds(pl.multiple_of(HEAD_DIM * h, 8), HEAD_DIM)] = got / total

    def attend_space(h):
        scores = scores_of(h)
        weights = jnp.exp2(scores - jnp.max(scores, axis=0, keepdims=True))
        total = jnp.sum(weights, axis=0, keepdims=True)
        mix(h, weights.astype(jnp.bfloat16), total)

    def attend_time(h):
        scores = scores_of(h)
        low = lax.broadcasted_iota(jnp.int32, (64, 128), 1) < 64
        near = jnp.concatenate(
            [
                jnp.where(low, scores[0:64, 0:128], scores[64:128, 0:128]),
                jnp.where(low, scores[128:192, 128:256], scores[192:256, 128:256]),
            ],
            axis=1,
        )
        weights = jnp.exp2(near - jnp.max(near, axis=0, keepdims=True))
        total = jnp.sum(weights, axis=0, keepdims=True)
        column = lax.broadcasted_iota(jnp.int32, (64, TOKENS), 1) // 64
        spread = jnp.concatenate([jnp.where(column == p, weights, 0.0) for p in range(4)], axis=0)
        mix(h, spread.astype(jnp.bfloat16), total)

    def project_out(layer, lo, hi_):
        first, offset = OUT_WINDOW[layer]

        def one(g, _):
            block = slots[pl.ds(8 * g, 8), pl.ds(first, 32)].reshape(256, WIDTH)
            got = jnp.dot(block, nt[...], preferred_element_type=jnp.float32).reshape(8, 32, TOKENS)
            got = jnp.concatenate([got[j, offset : offset + OUT_COLS] for j in range(8)], axis=0)
            at = pl.ds(pl.multiple_of(144 * g, 16), 144)
            ft[at] = (xt[at] + mod[at, 4 + layer : 5 + layer] * got).astype(jnp.bfloat16)
            return 0

        lax.fori_loop(lo, hi_, one, 0)

    def over_heads(attend, lo, hi_):
        def one(n, _):
            attend(lo + 2 * n)
            attend(lo + 2 * n + 1)
            return 0

        lax.fori_loop(0, (hi_ - lo) // 2, one, 0)

    done = {}
    for i, (k, dy, dz) in enumerate(order[:end_a]):
        if k in LAYER_PIECES[0]:
            done[dy, dz] = i
    blocks = sorted(done, key=done.get)
    batches = [blocks[n : n + 4] for n in range(0, 32, 4)]
    after = {}
    tasks = [functools.partial(make_sel_out, 0, q) for q in range(4)]
    tasks += [functools.partial(make_sel_in, 1, q) for q in range(3)]
    tasks += [functools.partial(make_sel_out, 1, q) for q in range(4)]
    tasks += [functools.partial(make_sel_in, 0, q) for q in range(3)]
    for n, task in enumerate([prepare] + tasks):
        after.setdefault(6 + 4 * n, []).append(task)

    def batch(n):
        ready = [block_of(core, dy, dz) for dy, dz in batches[n]] if n < 8 else []
        if n > 0:
            for dy, dz in batches[n - 1]:
                from_sibling(LAYER_PIECES[0], dy, dz)
                ready.append(block_of(other, dy, dz))
        project_slots(0, ready)

    for n in range(8):
        after.setdefault(max(done[block] for block in batches[n]), []).append(functools.partial(batch, n))
    for i in range(4, end_a):
        run(order[i : i + 1])
        for task in after.get(i, []):
            task()
    batch(8)

    rest = order[end_a:]

    def more(count):
        run(rest[:count])
        del rest[:count]

    for q in range(4):
        split_heads(0, 4 * q, 4 * q + 4)
        more(2)
    for q in range(8):
        over_heads(attend_space, 2 * q, 2 * q + 2)
        more(3)
    nt[...] = mixed[...].astype(jnp.bfloat16)
    for q in range(4):
        project_out(0, 2 * q, 2 * q + 2)
        more(3)
    pack_and_send(send_a, recv_a, 0)
    more(len(rest))
    for dy in range(4):
        for dz in range(8):
            from_sibling(LAYER_PIECES[1], dy, dz)
    exchanged(send_a, recv_a, 0)

    got = unpack(recv_a, 1)
    for t in range(3):
        xt[THIRD * t : THIRD * (t + 1)] = got[TOKENS * t : TOKENS * (t + 1)].T
    nt[...] = normalise(xt[...], mod[:, 1:2], mod[:, 3:4])
    project_qkv(1)
    split_heads(1, 0, 16)
    over_heads(attend_time, 0, HEADS)
    nt[...] = mixed[...].astype(jnp.bfloat16)
    project_out(1, 0, 8)
    pack_and_send(send_b, recv_b, 1)
    exchanged(send_b, recv_b, 1)
    got = unpack(recv_b, 0)
    for t in range(3):
        o_ref[:, THIRD * t : THIRD * (t + 1)] = got[TOKENS * t : TOKENS * (t + 1)].astype(jnp.bfloat16)

    def sent(k, way, count):
        rows = pl.ds(PIECES[k][0], PIECES[k][1])
        pltpu.make_async_remote_copy(
            src_ref=slots.at[pl.ds(0, count), rows], dst_ref=slots.at[pl.ds(0, count), rows],
            send_sem=ring_send.at[k, way], recv_sem=ring_recv.at[k, 0],
            device_id=sibling, device_id_type=MESH,
        ).wait_send()

    for k, piece in enumerate(PIECES):
        ways = [way for e in course(k) for way in routes(*e)]

        def plane_sent():
            for way in (UP_Y, DOWN_Y, UP_Z, DOWN_Z):
                sent(k, way, ways.count(way))

        if not piece[3]:
            plane_sent()

        @pl.when(hi == core)
        def _():
            if piece[3]:
                plane_sent()
            sent(k, OPPOSITE, 32 if piece[3] else 1)
            sent(k, SIBLING, 31)

        @pl.when(hi != core)
        def _():
            sent(k, SIBLING, 32)


def per_device(tokens, w_qkv, w_out, mod_shift, mod_scale, mod_gate):
    vmem = pl.BlockSpec(memory_space=pltpu.VMEM)
    result = pl.pallas_call(
        kernel,
        out_shape=jax.ShapeDtypeStruct((TOKENS, WIDTH), jnp.bfloat16),
        in_specs=[vmem] * 6,
        out_specs=vmem,
        scratch_shapes=[
            pltpu.VMEM((64, SLOT_ROWS, WIDTH), jnp.bfloat16),
            pltpu.VMEM((WIDTH, 8), jnp.float32),
            pltpu.VMEM((64, 64, TOKENS), jnp.float32),
            pltpu.VMEM((3 * HEADS, HEAD_DIM, TOKENS), jnp.bfloat16),
            pltpu.VMEM((WIDTH, TOKENS), jnp.float32),
            pltpu.VMEM((WIDTH, TOKENS), jnp.float32),
            pltpu.VMEM((WIDTH, TOKENS), jnp.bfloat16),
            pltpu.VMEM((WIDTH, TOKENS), jnp.bfloat16),
            pltpu.VMEM((2, 1024, 768), jnp.bfloat16),
            pltpu.VMEM((2, 768, 1024), jnp.bfloat16),
            pltpu.VMEM((64, 16, THIRD), jnp.bfloat16),
            pltpu.VMEM((64, 16, THIRD), jnp.bfloat16),
            pltpu.VMEM((64, 16, THIRD), jnp.bfloat16),
            pltpu.VMEM((64, 16, THIRD), jnp.bfloat16),
            pltpu.SemaphoreType.DMA((len(PIECES), 6)),
            pltpu.SemaphoreType.DMA((len(PIECES), 64)),
            pltpu.SemaphoreType.DMA((2,)),
            pltpu.SemaphoreType.DMA((2,)),
        ],
        compiler_params=pltpu.CompilerParams(
            collective_id=0, has_side_effects=True, vmem_limit_bytes=60 * 2**20
        ),
        name="latte",
    )(
        tokens.reshape(TOKENS, WIDTH),
        jnp.transpose(w_qkv, (2, 0, 1)),
        jnp.transpose(w_out, (2, 0, 1)),
        mod_shift,
        mod_scale,
        mod_gate,
    )
    return result.reshape(tokens.shape)


def solution(mesh):
    in_specs = (
        P("dp", "seq", None, None),
        P(None, None, "seq"),
        P(None, None, "seq"),
        P(),
        P(),
        P(),
    )
    return jax.shard_map(
        per_device, mesh=mesh, in_specs=in_specs, out_specs=P("dp", "seq", None, None), check_vma=False
    )
```

time: 206 us -> 148 us (0.72)
  Pallas kernels: 198 us -> 146 us
  local copies, waits for them, and re-layouts: 5.4 us -> 1.92 us
    pallas_call x1, Pallas kernels: 198 us -> 146 us  [per_device(): pl.pallas_call(kernel, out_shape=jax.ShapeDtypeStruct((TOKENS, WIDTH), jn...]
    unnamed x7 -> x1, local copies, waits for them, and re-layouts: 4.27 us -> 1.92 us
where the time goes in v2:
time: 148 us
  Pallas kernels  146 us (99%)
  local copies, waits for them, and re-layouts  1.92 us (1%)
    pallas_call x1, Pallas kernels, per_device(): pl.pallas_call(kernel, out_shape=jax.ShapeDtypeStruct((TOKENS, WIDTH), jn...  146 us

profile of v2, /device:TPU:39, one launch (start us, length us, event | category | flops | bytes accessed | tf_op | source)
XLA Modules:
  0.0 147.6 jit_solution(17533961457596566688)
XLA Ops:
  0.0 145.7 %latte.1 = bf16[256,1152]{1,0:T(8,128)(2,1)} custom-call(bf16[256,1152]{1,0:T(8,128)(2,1)} %bitcast.5, bf16[54,2,1152]{2,1,0:T(2,128)(2,1)} %bitcast.6, bf16[18,2,1152]{2,1,0:T(2,128)(2,1)} %bitcast.7, f32[2,1152]{1,0:T(2,128)} %shift_ref.1, f32[2,1152]{1,0:T(2,128)} %scale_ref.1, f32[2,1152]{1,0:T(2,128)} %gate_ref.1), custom_call_target="tpu_custom_call" | custom-call | tf_op jit(solution)/shard_map/latte/pallas_call | solution.py:447
  145.7 1.9 %copy.8 = bf16[1,1,256,1152]{3,2,1,0:T(8,128)(2,1)} copy(bf16[1,1,256,1152]{3,2,1,0:T(8,128)(2,1)} %bitcast.4) | data formatting | bytes 1179648

commit v3 on v2

--- a/solution.py
+++ b/solution.py
@@ -27,14 +27,14 @@
     (112, 16, "y", False),
     (128, 16, "y", True),
 )
-LAYER_PIECES = ((0, 1, 2, 3), (4, 5, 6))
+GROUPS = ((0, 1, 2, 3), (), (4, 5, 6))
 ORDER = (
-    32, 0, 64, 96, 33, 7, 71, 103, 1, 65, 24, 88, 39, 8, 56, 97, 40, 120, 72, 104, 6, 31, 2, 66,
-    70, 34, 63, 38, 102, 98, 57, 112, 89, 16, 95, 47, 73, 25, 79, 80, 41, 5, 15, 48, 3, 127, 121, 111,
-    30, 105, 67, 69, 14, 99, 10, 37, 35, 26, 94, 78, 58, 62, 101, 9, 23, 42, 46, 87, 49, 74, 122, 55,
-    90, 126, 4, 119, 59, 110, 13, 106, 68, 17, 11, 81, 43, 113, 36, 123, 50, 18, 77, 29, 107, 27, 75, 91,
-    100, 22, 60, 45, 54, 125, 86, 114, 61, 93, 82, 51, 28, 118, 12, 109, 21, 44, 53, 115, 76, 92, 19, 128,
-    83, 160, 117, 192, 108, 124, 85, 20, 52, 84, 116, 135, 129, 152, 136, 199, 193, 167, 161, 216, 200, 184, 168, 159,
+    32, 0, 64, 96, 33, 7, 71, 103, 1, 39, 88, 65, 24, 8, 97, 56, 120, 40, 72, 104, 6, 2, 31, 66,
+    70, 34, 63, 38, 98, 25, 57, 89, 112, 16, 102, 95, 47, 79, 80, 73, 41, 48, 15, 5, 3, 127, 121, 111,
+    30, 67, 14, 10, 26, 105, 37, 9, 69, 35, 94, 78, 23, 58, 62, 101, 42, 99, 46, 49, 90, 74, 122, 55,
+    126, 87, 119, 59, 110, 4, 81, 106, 113, 13, 68, 11, 17, 36, 22, 50, 29, 43, 123, 77, 18, 27, 91, 60,
+    100, 45, 75, 86, 54, 107, 114, 61, 93, 82, 51, 28, 118, 12, 109, 125, 21, 53, 115, 76, 19, 44, 128, 124,
+    160, 92, 192, 117, 83, 20, 85, 52, 108, 84, 116, 135, 129, 152, 136, 199, 193, 167, 161, 216, 200, 184, 168, 159,
     153, 143, 134, 130, 137, 198, 166, 162, 144, 194, 223, 217, 191, 185, 208, 207, 176, 201, 142, 175, 169, 151, 138, 145,
     158, 133, 131, 197, 163, 154, 195, 222, 165, 186, 218, 215, 209, 190, 177, 150, 206, 202, 157, 170, 146, 183, 155, 174,
     141, 139, 187, 196, 132, 219, 164, 178, 210, 189, 171, 149, 221, 203, 182, 147, 188, 214, 173, 205, 156, 179, 172, 140,
@@ -56,7 +56,7 @@
     x_ref, wqkv_ref, wout_ref, shift_ref, scale_ref, gate_ref, o_ref,
     slots, mod, qkv, heads, mixed, xt, nt, ft, sel_out, sel_in,
     send_a, recv_a, send_b, recv_b,
-    ring_send, ring_recv, a2a_send, a2a_recv,
+    ring_send, ring_recv, a2a_send, a2a_recv, entered,
 ):
     dp = lax.axis_index("dp")
     seq = lax.axis_index("seq")
@@ -69,17 +69,13 @@
 
     sibling = (2 * xlo + other, seq)
     opposite = (2 * (1 - xlo) + core, 32 * (1 - hi) + 4 * z + y)
+    beside = (2 * (1 - xlo) + core, seq)
     devices = (chip(y + 1, z), chip(y - 1, z), chip(y, z + 1), chip(y, z - 1), sibling, opposite)
 
     barrier = pltpu.get_barrier_semaphore()
 
-    def greet(k, _):
-        pl.semaphore_signal(barrier, inc=1, device_id=(dp, (seq + k) % 64), device_id_type=MESH)
-        return 0
-
-    lax.fori_loop(1, 64, greet, 0)
-    pl.semaphore_signal(barrier, inc=1, device_id=sibling, device_id_type=MESH)
-    pl.semaphore_signal(barrier, inc=1, device_id=opposite, device_id_type=MESH)
+    for device in (*devices, beside):
+        pl.semaphore_signal(barrier, inc=1, device_id=device, device_id_type=MESH)
 
     columns = wqkv_ref[...].astype(jnp.float32)
     outs = wout_ref[...].astype(jnp.float32)
@@ -87,7 +83,7 @@
     mine = 32 * hi + 4 * z + y
     slots[mine] = rows
 
-    pl.semaphore_wait(barrier, 65)
+    pl.semaphore_wait(barrier, 7)
 
     def part(slot, k):
         return slots.at[slot, pl.ds(PIECES[k][0], PIECES[k][1])]
@@ -190,8 +186,13 @@
         else:
             taken()
 
+    def all_from_sibling(ks):
+        for dy in range(4):
+            for dz in range(8):
+                from_sibling(ks, dy, dz)
+
     order = [(e // 32, e // 8 % 4, e % 8) for e in ORDER]
-    end_a = 1 + max(i for i, e in enumerate(order) if e[0] in LAYER_PIECES[0])
+    end_a = 1 + max(i for i, e in enumerate(order) if e[0] in GROUPS[0])
     run(order[:4])
 
     def prepare():
@@ -346,7 +347,7 @@
 
     done = {}
     for i, (k, dy, dz) in enumerate(order[:end_a]):
-        if k in LAYER_PIECES[0]:
+        if k in GROUPS[0]:
             done[dy, dz] = i
     blocks = sorted(done, key=done.get)
     batches = [blocks[n : n + 4] for n in range(0, 32, 4)]
@@ -362,7 +363,7 @@
         ready = [block_of(core, dy, dz) for dy, dz in batches[n]] if n < 8 else []
         if n > 0:
             for dy, dz in batches[n - 1]:
-                from_sibling(LAYER_PIECES[0], dy, dz)
+                from_sibling(GROUPS[0], dy, dz)
                 ready.append(block_of(other, dy, dz))
         project_slots(0, ready)
 
@@ -374,6 +375,11 @@
             task()
     batch(8)
 
+    def tell(n, device):
+        pl.semaphore_signal(entered.at[n], inc=1, device_id=device, device_id_type=MESH)
+
+    tell(0, opposite)
+
     rest = order[end_a:]
 
     def more(count):
@@ -382,19 +388,23 @@
 
     for q in range(4):
         split_heads(0, 4 * q, 4 * q + 4)
-        more(2)
+        more(4)
     for q in range(8):
         over_heads(attend_space, 2 * q, 2 * q + 2)
-        more(3)
+        more(5)
+    pl.semaphore_wait(entered.at[0], 1)
+    tell(1, beside)
+    if GROUPS[1]:
+        more(1 + max([i for i, e in enumerate(rest) if e[0] in GROUPS[1]], default=-1))
+        all_from_sibling(GROUPS[1])
     nt[...] = mixed[...].astype(jnp.bfloat16)
     for q in range(4):
         project_out(0, 2 * q, 2 * q + 2)
-        more(3)
+        more(4)
+    pl.semaphore_wait(entered.at[1], 1)
     pack_and_send(send_a, recv_a, 0)
     more(len(rest))
-    for dy in range(4):
-        for dz in range(8):
-            from_sibling(LAYER_PIECES[1], dy, dz)
+    all_from_sibling(GROUPS[2])
     exchanged(send_a, recv_a, 0)
 
     got = unpack(recv_a, 1)
@@ -468,6 +478,7 @@
             pltpu.SemaphoreType.DMA((len(PIECES), 64)),
             pltpu.SemaphoreType.DMA((2,)),
             pltpu.SemaphoreType.DMA((2,)),
+            pltpu.SemaphoreType.REGULAR((2,)),
         ],
         compiler_params=pltpu.CompilerParams(
             collective_id=0, has_side_effects=True, vmem_limit_bytes=60 * 2**20

time: 148 us -> 142 us (0.959)
  Pallas kernels: 146 us -> 140 us
    pallas_call x1, Pallas kernels: 146 us -> 140 us  [per_device(): pl.pallas_call(kernel, out_shape=jax.ShapeDtypeStruct((TOKENS, WIDTH), jn...]
where the time goes in v3:
time: 142 us
  Pallas kernels  140 us (99%)
  local copies, waits for them, and re-layouts  1.92 us (1%)
    pallas_call x1, Pallas kernels, per_device(): pl.pallas_call(kernel, out_shape=jax.ShapeDtypeStruct((TOKENS, WIDTH), jn...  140 us

profile of v3, /device:TPU:39, one launch (start us, length us, event | category | flops | bytes accessed | tf_op | source)
XLA Modules:
  0.0 141.6 jit_solution(16844586805642789333)
XLA Ops:
  0.0 139.7 %latte.1 = bf16[256,1152]{1,0:T(8,128)(2,1)} custom-call(bf16[256,1152]{1,0:T(8,128)(2,1)} %bitcast.5, bf16[54,2,1152]{2,1,0:T(2,128)(2,1)} %bitcast.6, bf16[18,2,1152]{2,1,0:T(2,128)(2,1)} %bitcast.7, f32[2,1152]{1,0:T(2,128)} %shift_ref.1, f32[2,1152]{1,0:T(2,128)} %scale_ref.1, f32[2,1152]{1,0:T(2,128)} %gate_ref.1), custom_call_target="tpu_custom_call" | custom-call | tf_op jit(solution)/shard_map/latte/pallas_call | solution.py:457
  139.7 1.9 %copy.8 = bf16[1,1,256,1152]{3,2,1,0:T(8,128)(2,1)} copy(bf16[1,1,256,1152]{3,2,1,0:T(8,128)(2,1)} %bitcast.4) | data formatting | bytes 1179648

commit v4 on v3

--- a/solution.py
+++ b/solution.py
@@ -11,7 +11,6 @@
 HEAD_DIM = 72
 WIDTH = 1152
 TOKENS = 256
-THIRD = WIDTH // 3
 LOG2E = 1.4426950408889634
 MESH = pl.DeviceIdType.MESH
 
@@ -24,7 +23,7 @@
     (48, 16, "z", True),
     (64, 16, "y", True),
     (80, 32, "z", False),
-    (112, 16, "y", False),
+    (112, 16, "z", True),
     (128, 16, "y", True),
 )
 GROUPS = ((0, 1, 2, 3), (), (4, 5, 6))
@@ -32,13 +31,13 @@
     32, 0, 64, 96, 33, 7, 71, 103, 1, 39, 88, 65, 24, 8, 97, 56, 120, 40, 72, 104, 6, 2, 31, 66,
     70, 34, 63, 38, 98, 25, 57, 89, 112, 16, 102, 95, 47, 79, 80, 73, 41, 48, 15, 5, 3, 127, 121, 111,
     30, 67, 14, 10, 26, 105, 37, 9, 69, 35, 94, 78, 23, 58, 62, 101, 42, 99, 46, 49, 90, 74, 122, 55,
-    126, 87, 119, 59, 110, 4, 81, 106, 113, 13, 68, 11, 17, 36, 22, 50, 29, 43, 123, 77, 18, 27, 91, 60,
-    100, 45, 75, 86, 54, 107, 114, 61, 93, 82, 51, 28, 118, 12, 109, 125, 21, 53, 115, 76, 19, 44, 128, 124,
-    160, 92, 192, 117, 83, 20, 85, 52, 108, 84, 116, 135, 129, 152, 136, 199, 193, 167, 161, 216, 200, 184, 168, 159,
-    153, 143, 134, 130, 137, 198, 166, 162, 144, 194, 223, 217, 191, 185, 208, 207, 176, 201, 142, 175, 169, 151, 138, 145,
-    158, 133, 131, 197, 163, 154, 195, 222, 165, 186, 218, 215, 209, 190, 177, 150, 206, 202, 157, 170, 146, 183, 155, 174,
-    141, 139, 187, 196, 132, 219, 164, 178, 210, 189, 171, 149, 221, 203, 182, 147, 188, 214, 173, 205, 156, 179, 172, 140,
-    211, 181, 220, 213, 204, 212, 148, 180,
+    126, 87, 119, 128, 160, 59, 110, 4, 81, 106, 192, 113, 13, 68, 11, 17, 36, 22, 50, 29, 43, 123, 77, 18,
+    27, 91, 135, 60, 100, 129, 152, 45, 136, 167, 75, 161, 86, 54, 184, 107, 168, 114, 61, 199, 93, 193, 82, 51,
+    216, 28, 118, 12, 200, 109, 134, 130, 125, 159, 21, 166, 53, 115, 76, 162, 153, 143, 19, 44, 124, 198, 92, 194,
+    137, 117, 223, 83, 20, 217, 144, 85, 191, 133, 131, 52, 108, 207, 84, 201, 116, 185, 176, 175, 169, 208, 158, 132,
+    165, 142, 163, 154, 197, 138, 195, 151, 222, 218, 206, 202, 215, 209, 164, 190, 145, 141, 196, 186, 157, 139, 221, 219,
+    155, 174, 205, 203, 170, 183, 210, 214, 156, 140, 220, 177, 150, 204, 211, 146, 213, 189, 149, 173, 187, 147, 171, 212,
+    148, 188, 172, 182, 178, 181, 179, 180,
 )
 UP_Y, DOWN_Y, UP_Z, DOWN_Z, SIBLING, OPPOSITE = range(6)
 QKV_WINDOW = ((0, 0), (80, 10))
@@ -55,9 +54,10 @@
 def kernel(
     x_ref, wqkv_ref, wout_ref, shift_ref, scale_ref, gate_ref, o_ref,
     slots, mod, qkv, heads, mixed, xt, nt, ft, sel_out, sel_in,
-    send_a, recv_a, send_b, recv_b,
-    ring_send, ring_recv, a2a_send, a2a_recv, entered,
+    tail, *rest_refs,
 ):
+    bufs_a, bufs_b = rest_refs[:6], rest_refs[6:12]
+    ring_send, ring_recv, a2a_send, a2a_recv, tail_sem, entered = rest_refs[12:]
     dp = lax.axis_index("dp")
     seq = lax.axis_index("seq")
     core, xlo = dp % 2, dp // 2
@@ -201,24 +201,57 @@
         xt[...] = x_ref[...].astype(jnp.float32).T
         nt[...] = normalise(xt[...], mod[:, 0:1], mod[:, 2:3])
 
-    def selected(shape, axis, start, by_frame):
-        packed = lax.broadcasted_iota(jnp.int32, shape, axis) + start
-        s, t, p = packed >> 4, (packed >> 2) & 3, packed & 3
-        at = 256 * t + (64 * p + s if by_frame else 4 * s + p)
-        return jnp.where(t < 3, at, -1)
+    def token_at(by_frame, s, p):
+        return 64 * p + s if by_frame else 4 * s + p
+
+    def permutation(rows, cols):
+        return jnp.where(rows == cols, 1.0, 0.0).astype(jnp.bfloat16)
 
     def make_sel_out(by_frame, q):
-        at = selected((256, 1), 0, 256 * q, by_frame)
-        token = lax.broadcasted_iota(jnp.int32, (256, 768), 1)
-        sel_out[by_frame, 256 * q : 256 * (q + 1)] = jnp.where(at == token, 1.0, 0.0).astype(jnp.bfloat16)
+        row = lax.broadcasted_iota(jnp.int32, (256, 1), 0) + 256 * q
+        want = 256 * ((row >> 2) & 3) + token_at(by_frame, row >> 4, row & 3)
+        sel_out[by_frame, 256 * q : 256 * (q + 1)] = permutation(
+            want, lax.broadcasted_iota(jnp.int32, (256, 1024), 1)
+        )
 
     def make_sel_in(by_frame, q):
-        at = selected((1, 1024), 1, 0, by_frame)
-        token = lax.broadcasted_iota(jnp.int32, (256, 1024), 0) + 256 * q
-        sel_in[by_frame, 256 * q : 256 * (q + 1)] = jnp.where(at == token, 1.0, 0.0).astype(jnp.bfloat16)
-
-    def pack_and_send(send_ref, recv_ref, by_frame):
-        flat = jnp.concatenate([ft[0:THIRD], ft[THIRD : 2 * THIRD], ft[2 * THIRD :]], axis=1)
+        col = lax.broadcasted_iota(jnp.int32, (1, 1024), 1)
+        want = 256 * ((col >> 2) & 3) + token_at(by_frame, col >> 4, col & 3)
+        sel_in[by_frame, 256 * q : 256 * (q + 1)] = permutation(
+            lax.broadcasted_iota(jnp.int32, (256, 1024), 0) + 256 * q, want
+        )
+
+    def make_tail():
+        row = lax.broadcasted_iota(jnp.int32, (256, 1), 0)
+        col = lax.broadcasted_iota(jnp.int32, (1, 256), 1)
+        rows = lax.broadcasted_iota(jnp.int32, (256, 256), 0)
+        cols = lax.broadcasted_iota(jnp.int32, (256, 256), 1)
+        for by_frame in (0, 1):
+            tail[by_frame] = permutation(token_at(by_frame, row >> 2, row & 3), cols)
+            sender = 4 * ((col >> 2) & 15) + (col >> 6)
+            tail[2 + by_frame] = permutation(rows, token_at(by_frame, sender, col & 3))
+        tail[4] = permutation(16 * ((row >> 2) & 15) + 4 * (row >> 6) + (row & 3), cols)
+
+    def pack_and_send(bufs, by_frame):
+        send_ref, recv_ref, line_out, line_in, _, _ = bufs
+        line = seq // 4
+        got = lax.dot_general(
+            tail[by_frame], ft[1024:], (((1,), (1,)), ((), ())), preferred_element_type=jnp.float32
+        )
+        line_out[...] = got.astype(jnp.bfloat16).reshape(16, 16, 128)
+
+        def along(k, _):
+            to = lax.rem(line + k, 16)
+            pltpu.make_async_remote_copy(
+                src_ref=line_out.at[to], dst_ref=line_in.at[line],
+                send_sem=tail_sem.at[0, by_frame], recv_sem=tail_sem.at[1, by_frame],
+                device_id=(dp, 4 * to + y), device_id_type=MESH,
+            ).start()
+            return 0
+
+        lax.fori_loop(1, 16, along, 0)
+        line_in[line] = line_out[line]
+        flat = jnp.concatenate([ft[256 * t : 256 * (t + 1)] for t in range(4)], axis=1)
 
         def quarter(c, _):
             q = lax.rem(seq // 16 + 1 + c, 4)
@@ -226,7 +259,7 @@
                 sel_out[by_frame, pl.ds(pl.multiple_of(256 * q, 256), 256)], flat,
                 (((1,), (1,)), ((), ())), preferred_element_type=jnp.float32,
             )
-            send_ref[pl.ds(16 * q, 16)] = packed.astype(jnp.bfloat16).reshape(16, 16, THIRD)
+            send_ref[pl.ds(16 * q, 16)] = packed.astype(jnp.bfloat16).reshape(16, 16, 256)
 
             def one(j, _):
                 to = 16 * q + lax.rem(seq + j, 16)
@@ -247,19 +280,39 @@
         lax.fori_loop(0, 4, quarter, 0)
         recv_ref[seq] = send_ref[seq]
 
-    def unpack(recv_ref, by_frame):
-        return jnp.dot(
-            sel_in[by_frame], recv_ref[...].reshape(1024, THIRD), preferred_element_type=jnp.float32
-        )
-
-    def exchanged(send_ref, recv_ref, which):
+    def relay(bufs, by_frame):
+        _, _, line_out, line_in, y_out, y_in = bufs
+        line = seq // 4
+        finish(line_out.at[pl.ds(0, 15)], line_in.at[pl.ds(0, 15)], tail_sem.at[0, by_frame], tail_sem.at[1, by_frame])
+        got = jnp.dot(tail[4], line_in[...].reshape(256, 128), preferred_element_type=jnp.float32)
+        y_out[...] = got.astype(jnp.bfloat16).reshape(4, 64, 128)
+        for k in range(1, 4):
+            to = lax.rem(y + k, 4)
+            pltpu.make_async_remote_copy(
+                src_ref=y_out.at[to], dst_ref=y_in.at[y],
+                send_sem=tail_sem.at[2, by_frame], recv_sem=tail_sem.at[3, by_frame],
+                device_id=(dp, 4 * line + to), device_id_type=MESH,
+            ).start()
+        y_in[y] = y_out[y]
+
+    def finish(src, dst, send, recv):
         done = pltpu.make_async_remote_copy(
-            src_ref=send_ref.at[pl.ds(0, 63)], dst_ref=recv_ref.at[pl.ds(0, 63)],
-            send_sem=a2a_send.at[which], recv_sem=a2a_recv.at[which],
-            device_id=sibling, device_id_type=MESH,
+            src_ref=src, dst_ref=dst, send_sem=send, recv_sem=recv, device_id=sibling, device_id_type=MESH
         )
         done.wait_send()
         done.wait_recv()
+
+    def exchanged(bufs, by_frame):
+        send_ref, recv_ref, _, _, y_out, y_in = bufs
+        finish(y_out.at[pl.ds(0, 3)], y_in.at[pl.ds(0, 3)], tail_sem.at[2, by_frame], tail_sem.at[3, by_frame])
+        finish(send_ref.at[pl.ds(0, 63)], recv_ref.at[pl.ds(0, 63)], a2a_send.at[by_frame], a2a_recv.at[by_frame])
+
+    def unpack(bufs, by_frame):
+        main = jnp.dot(
+            sel_in[by_frame], bufs[1][...].reshape(1024, 256), preferred_element_type=jnp.float32
+        )
+        last = jnp.dot(tail[2 + by_frame], bufs[5][...].reshape(256, 128), preferred_element_type=jnp.float32)
+        return [main[256 * t : 256 * (t + 1)] for t in range(4)] + [last]
 
     def project_slots(layer, slot_list):
         first = QKV_WINDOW[layer][0]
@@ -337,13 +390,13 @@
 
         lax.fori_loop(lo, hi_, one, 0)
 
-    def over_heads(attend, lo, hi_):
+    def over_heads(attend, lo, hi_, step=2):
         def one(n, _):
-            attend(lo + 2 * n)
-            attend(lo + 2 * n + 1)
+            for j in range(step):
+                attend(lo + step * n + j)
             return 0
 
-        lax.fori_loop(0, (hi_ - lo) // 2, one, 0)
+        lax.fori_loop(0, (hi_ - lo) // step, one, 0)
 
     done = {}
     for i, (k, dy, dz) in enumerate(order[:end_a]):
@@ -352,10 +405,10 @@
     blocks = sorted(done, key=done.get)
     batches = [blocks[n : n + 4] for n in range(0, 32, 4)]
     after = {}
-    tasks = [functools.partial(make_sel_out, 0, q) for q in range(4)]
-    tasks += [functools.partial(make_sel_in, 1, q) for q in range(3)]
-    tasks += [functools.partial(make_sel_out, 1, q) for q in range(4)]
-    tasks += [functools.partial(make_sel_in, 0, q) for q in range(3)]
+    tasks = [make_tail]
+    for by_frame in (0, 1):
+        tasks += [functools.partial(make_sel_out, by_frame, q) for q in range(4)]
+        tasks += [functools.partial(make_sel_in, 1 - by_frame, q) for q in range(4)]
     for n, task in enumerate([prepare] + tasks):
         after.setdefault(6 + 4 * n, []).append(task)
 
@@ -388,10 +441,10 @@
 
     for q in range(4):
         split_heads(0, 4 * q, 4 * q + 4)
-        more(4)
+        more(2)
     for q in range(8):
         over_heads(attend_space, 2 * q, 2 * q + 2)
-        more(5)
+        more(2)
     pl.semaphore_wait(entered.at[0], 1)
     tell(1, beside)
     if GROUPS[1]:
@@ -400,27 +453,28 @@
     nt[...] = mixed[...].astype(jnp.bfloat16)
     for q in range(4):
         project_out(0, 2 * q, 2 * q + 2)
-        more(4)
+        more(2)
     pl.semaphore_wait(entered.at[1], 1)
-    pack_and_send(send_a, recv_a, 0)
+    pack_and_send(bufs_a, 0)
+    more(len(rest) // 2)
+    relay(bufs_a, 0)
     more(len(rest))
     all_from_sibling(GROUPS[2])
-    exchanged(send_a, recv_a, 0)
-
-    got = unpack(recv_a, 1)
-    for t in range(3):
-        xt[THIRD * t : THIRD * (t + 1)] = got[TOKENS * t : TOKENS * (t + 1)].T
+    exchanged(bufs_a, 0)
+
+    for t, got in enumerate(unpack(bufs_a, 1)):
+        xt[256 * t : 256 * t + got.shape[1]] = got.T
     nt[...] = normalise(xt[...], mod[:, 1:2], mod[:, 3:4])
     project_qkv(1)
     split_heads(1, 0, 16)
-    over_heads(attend_time, 0, HEADS)
+    over_heads(attend_time, 0, HEADS, 4)
     nt[...] = mixed[...].astype(jnp.bfloat16)
     project_out(1, 0, 8)
-    pack_and_send(send_b, recv_b, 1)
-    exchanged(send_b, recv_b, 1)
-    got = unpack(recv_b, 0)
-    for t in range(3):
-        o_ref[:, THIRD * t : THIRD * (t + 1)] = got[TOKENS * t : TOKENS * (t + 1)].astype(jnp.bfloat16)
+    pack_and_send(bufs_b, 1)
+    relay(bufs_b, 1)
+    exchanged(bufs_b, 1)
+    for t, got in enumerate(unpack(bufs_b, 0)):
+        o_ref[:, 256 * t : 256 * t + got.shape[1]] = got.astype(jnp.bfloat16)
 
     def sent(k, way, count):
         rows = pl.ds(PIECES[k][0], PIECES[k][1])
@@ -454,6 +508,10 @@
 
 def per_device(tokens, w_qkv, w_out, mod_shift, mod_scale, mod_gate):
     vmem = pl.BlockSpec(memory_space=pltpu.VMEM)
+    exchange_buffers = [
+        pltpu.VMEM(shape, jnp.bfloat16)
+        for shape in ((64, 16, 256), (64, 16, 256), (16, 16, 128), (16, 16, 128), (4, 64, 128), (4, 64, 128))
+    ]
     result = pl.pallas_call(
         kernel,
         out_shape=jax.ShapeDtypeStruct((TOKENS, WIDTH), jnp.bfloat16),
@@ -468,16 +526,16 @@
             pltpu.VMEM((WIDTH, TOKENS), jnp.float32),
             pltpu.VMEM((WIDTH, TOKENS), jnp.bfloat16),
             pltpu.VMEM((WIDTH, TOKENS), jnp.bfloat16),
-            pltpu.VMEM((2, 1024, 768), jnp.bfloat16),
-            pltpu.VMEM((2, 768, 1024), jnp.bfloat16),
-            pltpu.VMEM((64, 16, THIRD), jnp.bfloat16),
-            pltpu.VMEM((64, 16, THIRD), jnp.bfloat16),
-            pltpu.VMEM((64, 16, THIRD), jnp.bfloat16),
-            pltpu.VMEM((64, 16, THIRD), jnp.bfloat16),
+            pltpu.VMEM((2, 1024, 1024), jnp.bfloat16),
+            pltpu.VMEM((2, 1024, 1024), jnp.bfloat16),
+            pltpu.VMEM((5, 256, 256), jnp.bfloat16),
+            *exchange_buffers,
+            *exchange_buffers,
             pltpu.SemaphoreType.DMA((len(PIECES), 6)),
             pltpu.SemaphoreType.DMA((len(PIECES), 64)),
             pltpu.SemaphoreType.DMA((2,)),
             pltpu.SemaphoreType.DMA((2,)),
+            pltpu.SemaphoreType.DMA((4, 2)),
             pltpu.SemaphoreType.REGULAR((2,)),
         ],
         compiler_params=pltpu.CompilerParams(

time: 142 us -> 127 us (0.89)
  Pallas kernels: 140 us -> 124 us
    pallas_call x1, Pallas kernels: 140 us -> 124 us  [per_device(): pl.pallas_call(kernel, out_shape=jax.ShapeDtypeStruct((TOKENS, WIDTH), jn...]
where the time goes in v4:
time: 127 us; the launch traced here: 126 us
  Pallas kernels  124 us (98%)
  local copies, waits for them, and re-layouts  1.92 us (2%)
    pallas_call x1, Pallas kernels, per_device(): pl.pallas_call(kernel, out_shape=jax.ShapeDtypeStruct((TOKENS, WIDTH), jn...  124 us

profile of v4, /device:TPU:39, one launch (start us, length us, event | category | flops | bytes accessed | tf_op | source)
XLA Modules:
  0.0 126.3 jit_solution(8946358120106403940)
XLA Ops:
  0.0 124.3 %latte.1 = bf16[256,1152]{1,0:T(8,128)(2,1)} custom-call(bf16[256,1152]{1,0:T(8,128)(2,1)} %bitcast.5, bf16[54,2,1152]{2,1,0:T(2,128)(2,1)} %bitcast.6, bf16[18,2,1152]{2,1,0:T(2,128)(2,1)} %bitcast.7, f32[2,1152]{1,0:T(2,128)} %shift_ref.1, f32[2,1152]{1,0:T(2,128)} %scale_ref.1, f32[2,1152]{1,0:T(2,128)} %gate_ref.1), custom_call_target="tpu_custom_call" | custom-call | tf_op jit(solution)/shard_map/latte/pallas_call | solution.py:515
  124.3 1.9 %copy.8 = bf16[1,1,256,1152]{3,2,1,0:T(8,128)(2,1)} copy(bf16[1,1,256,1152]{3,2,1,0:T(8,128)(2,1)} %bitcast.4) | data formatting | bytes 1179648

commit v5 on v4

--- a/solution.py
+++ b/solution.py
@@ -232,7 +232,7 @@
             tail[2 + by_frame] = permutation(rows, token_at(by_frame, sender, col & 3))
         tail[4] = permutation(16 * ((row >> 2) & 15) + 4 * (row >> 6) + (row & 3), cols)
 
-    def pack_and_send(bufs, by_frame):
+    def pack_and_send(bufs, by_frame, between=None):
         send_ref, recv_ref, line_out, line_in, _, _ = bufs
         line = seq // 4
         got = lax.dot_general(
@@ -277,7 +277,12 @@
             lax.fori_loop(0, 16, one, 0)
             return 0
 
-        lax.fori_loop(0, 4, quarter, 0)
+        if between is None:
+            lax.fori_loop(0, 4, quarter, 0)
+        else:
+            for c in range(4):
+                between()
+                quarter(c, 0)
         recv_ref[seq] = send_ref[seq]
 
     def relay(bufs, by_frame):
@@ -408,7 +413,7 @@
     tasks = [make_tail]
     for by_frame in (0, 1):
         tasks += [functools.partial(make_sel_out, by_frame, q) for q in range(4)]
-        tasks += [functools.partial(make_sel_in, 1 - by_frame, q) for q in range(4)]
+    tasks += [functools.partial(make_sel_in, 0, q) for q in range(4)]
     for n, task in enumerate([prepare] + tasks):
         after.setdefault(6 + 4 * n, []).append(task)
 
@@ -455,15 +460,21 @@
         project_out(0, 2 * q, 2 * q + 2)
         more(2)
     pl.semaphore_wait(entered.at[1], 1)
-    pack_and_send(bufs_a, 0)
+    pack_and_send(bufs_a, 0, functools.partial(more, 4))
     more(len(rest) // 2)
     relay(bufs_a, 0)
     more(len(rest))
     all_from_sibling(GROUPS[2])
     exchanged(bufs_a, 0)
 
-    for t, got in enumerate(unpack(bufs_a, 1)):
-        xt[256 * t : 256 * t + got.shape[1]] = got.T
+    got = lax.dot_general(
+        bufs_a[1][...].reshape(1024, 256), sel_out[1],
+        (((0,), (0,)), ((), ())), preferred_element_type=jnp.float32,
+    )
+    for t in range(4):
+        xt[256 * t : 256 * (t + 1)] = got[:, 256 * t : 256 * (t + 1)]
+    last = jnp.dot(tail[3], bufs_a[5][...].reshape(256, 128), preferred_element_type=jnp.float32)
+    xt[1024:] = last.T
     nt[...] = normalise(xt[...], mod[:, 1:2], mod[:, 3:4])
     project_qkv(1)
     split_heads(1, 0, 16)
@@ -527,7 +538,7 @@
             pltpu.VMEM((WIDTH, TOKENS), jnp.bfloat16),
             pltpu.VMEM((WIDTH, TOKENS), jnp.bfloat16),
             pltpu.VMEM((2, 1024, 1024), jnp.bfloat16),
-            pltpu.VMEM((2, 1024, 1024), jnp.bfloat16),
+            pltpu.VMEM((1, 1024, 1024), jnp.bfloat16),
             pltpu.VMEM((5, 256, 256), jnp.bfloat16),
             *exchange_buffers,
             *exchange_buffers,

time: 127 us -> 124 us (0.976)
  Pallas kernels: 124 us -> 121 us
    pallas_call x1, Pallas kernels: 124 us -> 121 us  [per_device(): pl.pallas_call(kernel, out_shape=jax.ShapeDtypeStruct((TOKENS, WIDTH), jn...]
where the time goes in v5:
time: 124 us; the launch traced here: 123 us
  Pallas kernels  121 us (98%)
  local copies, waits for them, and re-layouts  1.92 us (2%)
    pallas_call x1, Pallas kernels, per_device(): pl.pallas_call(kernel, out_shape=jax.ShapeDtypeStruct((TOKENS, WIDTH), jn...  121 us

profile of v5, /device:TPU:39, one launch (start us, length us, event | category | flops | bytes accessed | tf_op | source)
XLA Modules:
  0.0 122.6 jit_solution(16078071746438471032)
XLA Ops:
  0.0 120.6 %latte.1 = bf16[256,1152]{1,0:T(8,128)(2,1)} custom-call(bf16[256,1152]{1,0:T(8,128)(2,1)} %bitcast.5, bf16[54,2,1152]{2,1,0:T(2,128)(2,1)} %bitcast.6, bf16[18,2,1152]{2,1,0:T(2,128)(2,1)} %bitcast.7, f32[2,1152]{1,0:T(2,128)} %shift_ref.1, f32[2,1152]{1,0:T(2,128)} %scale_ref.1, f32[2,1152]{1,0:T(2,128)} %gate_ref.1), custom_call_target="tpu_custom_call" | custom-call | tf_op jit(solution)/shard_map/latte/pallas_call | solution.py:526
  120.7 1.9 %copy.8 = bf16[1,1,256,1152]{3,2,1,0:T(8,128)(2,1)} copy(bf16[1,1,256,1152]{3,2,1,0:T(8,128)(2,1)} %bitcast.4) | data formatting | bytes 1179648

commit v6 on v5

--- a/solution.py
+++ b/solution.py
@@ -28,13 +28,13 @@
 )
 GROUPS = ((0, 1, 2, 3), (), (4, 5, 6))
 ORDER = (
-    32, 0, 64, 96, 33, 7, 71, 103, 1, 39, 88, 65, 24, 8, 97, 56, 120, 40, 72, 104, 6, 2, 31, 66,
-    70, 34, 63, 38, 98, 25, 57, 89, 112, 16, 102, 95, 47, 79, 80, 73, 41, 48, 15, 5, 3, 127, 121, 111,
-    30, 67, 14, 10, 26, 105, 37, 9, 69, 35, 94, 78, 23, 58, 62, 101, 42, 99, 46, 49, 90, 74, 122, 55,
-    126, 87, 119, 128, 160, 59, 110, 4, 81, 106, 192, 113, 13, 68, 11, 17, 36, 22, 50, 29, 43, 123, 77, 18,
-    27, 91, 135, 60, 100, 129, 152, 45, 136, 167, 75, 161, 86, 54, 184, 107, 168, 114, 61, 199, 93, 193, 82, 51,
-    216, 28, 118, 12, 200, 109, 134, 130, 125, 159, 21, 166, 53, 115, 76, 162, 153, 143, 19, 44, 124, 198, 92, 194,
-    137, 117, 223, 83, 20, 217, 144, 85, 191, 133, 131, 52, 108, 207, 84, 201, 116, 185, 176, 175, 169, 208, 158, 132,
+    0, 64, 32, 96, 7, 1, 65, 33, 71, 39, 56, 40, 72, 103, 97, 120, 8, 6, 31, 104, 2, 15, 24, 88,
+    38, 66, 25, 70, 34, 102, 57, 63, 95, 98, 89, 121, 73, 41, 47, 79, 9, 127, 80, 48, 111, 112, 105, 5,
+    37, 14, 23, 16, 69, 35, 3, 10, 99, 67, 58, 78, 42, 101, 62, 87, 30, 46, 94, 74, 26, 17, 49, 90,
+    55, 126, 122, 110, 113, 59, 128, 4, 119, 160, 106, 192, 81, 11, 43, 50, 13, 75, 29, 36, 114, 18, 86, 27,
+    68, 123, 61, 135, 129, 152, 136, 167, 77, 22, 161, 100, 60, 184, 107, 54, 168, 44, 93, 199, 91, 45, 193, 125,
+    51, 28, 216, 118, 12, 200, 82, 134, 130, 124, 159, 21, 115, 166, 53, 162, 153, 143, 19, 108, 76, 198, 92, 194,
+    137, 117, 223, 109, 217, 144, 85, 191, 133, 131, 83, 20, 52, 207, 84, 201, 116, 185, 176, 175, 169, 208, 158, 132,
     165, 142, 163, 154, 197, 138, 195, 151, 222, 218, 206, 202, 215, 209, 164, 190, 145, 141, 196, 186, 157, 139, 221, 219,
     155, 174, 205, 203, 170, 183, 210, 214, 156, 140, 220, 177, 150, 204, 211, 146, 213, 189, 149, 173, 187, 147, 171, 212,
     148, 188, 172, 182, 178, 181, 179, 180,

time: 124 us -> 124 us (level)
  no operation moved by 1% of the time
where the time goes in v6:
time: 124 us; the launch traced here: 122 us
  Pallas kernels  120 us (97%)
  local copies, waits for them, and re-layouts  1.92 us (2%)
    pallas_call x1, Pallas kernels, per_device(): pl.pallas_call(kernel, out_shape=jax.ShapeDtypeStruct((TOKENS, WIDTH), jn...  120 us

profile of v6, /device:TPU:39, one launch (start us, length us, event | category | flops | bytes accessed | tf_op | source)
XLA Modules:
  0.0 122.3 jit_solution(16560504576205381835)
XLA Ops:
  0.0 120.4 %latte.1 = bf16[256,1152]{1,0:T(8,128)(2,1)} custom-call(bf16[256,1152]{1,0:T(8,128)(2,1)} %bitcast.5, bf16[54,2,1152]{2,1,0:T(2,128)(2,1)} %bitcast.6, bf16[18,2,1152]{2,1,0:T(2,128)(2,1)} %bitcast.7, f32[2,1152]{1,0:T(2,128)} %shift_ref.1, f32[2,1152]{1,0:T(2,128)} %scale_ref.1, f32[2,1152]{1,0:T(2,128)} %gate_ref.1), custom_call_target="tpu_custom_call" | custom-call | tf_op jit(solution)/shard_map/latte/pallas_call | solution.py:526
  120.4 1.9 %copy.8 = bf16[1,1,256,1152]{3,2,1,0:T(8,128)(2,1)} copy(bf16[1,1,256,1152]{3,2,1,0:T(8,128)(2,1)} %bitcast.4) | data formatting | bytes 1179648
